TPU v7x, 256 devices: a whole 4x4x8 slice. The times are simulated.
256 devices in a mesh: grp: 4 (over y_lo, core), dom: 64 (over x, y_hi, z).
Axes of the slice: x: 4, y: 4 (y_hi: 2, y_lo: 2; y = y_hi * 2 + y_lo), z: 8, core: 2. Of those that a mesh axis runs over, the one named last changes fastest.
Arguments:
- left_table: float32 [262144, 256], P(('grp', 'dom')), may hold values from -1.5 to 1.5
- left_state: float32 [262144], P(('grp', 'dom')), may hold values from 0.001 to 0.1
- right_table: float32 [262144, 256], P(('grp', 'dom')), may hold values from -1.5 to 1.5
- right_state: float32 [262144], P(('grp', 'dom')), may hold values from 0.001 to 0.1
- operators: float32 [2304, 256], P(('grp', 'dom')), may hold values from 0.1 to 1.9
- operator_state: float32 [2304, 256], P(('grp', 'dom')), may hold values from 0.01 to 1
- heads: int32 [2, 1048576], P(None, ('grp', 'dom')), may hold values from 0 to 1023
- tails: int32 [2, 1048576], P(None, ('grp', 'dom')), may hold values from 0 to 1023
- relations: int32 [2, 1048576], P(None, ('grp', 'dom')), may hold values from 0 to 2303
- negatives: int32 [2, 2048, 512], P(None, ('grp', 'dom')), may hold values from 0 to 1023
- edge_counts: int32 [2, 256], P(None, ('grp', 'dom')), may hold values from 1 to 4096, 524288 in all within a row
- partner_mask: int32 [1], replicated, may hold values from 1 to 63
Outputs:
- new_left_table: float32 [262144, 256], P(('grp', 'dom'))
- new_left_state: float32 [262144], P(('grp', 'dom'))
- new_right_table: float32 [262144, 256], P(('grp', 'dom'))
- new_right_state: float32 [262144], P(('grp', 'dom'))
- new_operators: float32 [2304, 256], P(('grp', 'dom'))
Inputs may be any that keep to these rules, and one draw needn't show every extreme that they name: `edge_counts`: in each round some bucket has exactly 4096 live edges.
All inputs are finite; a program needn't handle non-finite values. No bound on the sum of `edge_counts` on one device may be relied on, other than what follows from the above.
Results may differ from a plain program's by a relative error of at most 0.0003.
Values sent between devices are 32-bit elements; how exact they have to be, the bound alone decides.
No kernel may reach another device: no remote copies, remote signals or barrier semaphores. Data moves between devices by JAX's collectives and lax.ppermute only.
A program may use at most 64 MiB of HBM per device.

v0:
```python
import jax
import jax.numpy as jnp
from jax import lax
from jax.sharding import PartitionSpec as P

embed_rate = 0.1
operator_rate = 0.5
highest = lax.Precision.HIGHEST


def swapped(x, axis, distance):
    return lax.ppermute(x, axis, [(i, i ^ 1 << distance) for i in range(lax.axis_size(axis))])


def block_update(carried, head_index, tail_index, rel_index, neg_index, edge_mask, operator_rows):
    left_part, left_acc, right_part, right_acc, rel_grads = carried
    head_rows = left_part[head_index]
    tail_rows = right_part[tail_index]
    neg_rows = right_part[neg_index]
    diag_rows = operator_rows[rel_index]
    scaled_heads = head_rows * diag_rows
    positive = jnp.sum(scaled_heads * tail_rows, axis=1)
    negative = jnp.einsum("cd,nd->cn", scaled_heads, neg_rows, precision=highest)
    pos_grad = -jax.nn.sigmoid(-positive) * edge_mask
    neg_grad = jax.nn.sigmoid(negative) * (edge_mask / neg_index.shape[0])[:, None]
    head_side = pos_grad[:, None] * tail_rows + jnp.dot(neg_grad, neg_rows, precision=highest)
    tail_side = pos_grad[:, None] * scaled_heads
    neg_side = jnp.einsum("cn,cd->nd", neg_grad, scaled_heads, precision=highest)
    left_grad = jnp.zeros_like(left_part).at[head_index].add(head_side * diag_rows)
    right_grad = (
        jnp.zeros_like(right_part).at[tail_index].add(tail_side).at[neg_index].add(neg_side)
    )
    rel_grads = rel_grads.at[rel_index].add(head_side * head_rows)
    left_acc = left_acc + jnp.mean(left_grad * left_grad, axis=1)
    left_part = left_part - embed_rate * left_grad / jnp.sqrt(left_acc)[:, None]
    right_acc = right_acc + jnp.mean(right_grad * right_grad, axis=1)
    right_part = right_part - embed_rate * right_grad / jnp.sqrt(right_acc)[:, None]
    return (left_part, left_acc, right_part, right_acc, rel_grads)


def train_bucket(carried, head_list, tail_list, rel_list, neg_list, edge_count, operator_rows):
    block_rows = head_list.shape[0] // neg_list.shape[0]

    def one_block(block_index, state_tuple):
        start = block_index * block_rows
        head_index = lax.dynamic_slice_in_dim(head_list, start, block_rows)
        tail_index = lax.dynamic_slice_in_dim(tail_list, start, block_rows)
        rel_index = lax.dynamic_slice_in_dim(rel_list, start, block_rows)
        neg_index = lax.dynamic_index_in_dim(neg_list, block_index, 0, keepdims=False)
        positions = start + jnp.arange(block_rows, dtype=jnp.int32)
        edge_mask = (positions < edge_count).astype(jnp.float32)
        return block_update(
            state_tuple, head_index, tail_index, rel_index, neg_index, edge_mask, operator_rows
        )

    turns = (edge_count + block_rows - 1) // block_rows
    return lax.fori_loop(0, turns, one_block, carried)


def relocate(payload, mask_value, bit_order):
    for bit_index in bit_order:
        selected = mask_value >> bit_index & 1 == 1
        arrived = swapped((payload[0], payload[1]), "dom", bit_index)
        payload = (
            jnp.where(selected, arrived[0], payload[0]),
            jnp.where(selected, arrived[1], payload[1]),
        )
    return payload


def body(
    left_table,
    left_state,
    right_table,
    right_state,
    operators,
    operator_state,
    heads,
    tails,
    relations,
    negatives,
    edge_counts,
    partner_mask,
):
    operator_rows = lax.all_gather(operators, ("grp", "dom"), axis=0, tiled=True)
    zero_grads = jnp.zeros(operator_rows.shape, jnp.float32)
    first_pass = train_bucket(
        (left_table, left_state, right_table, right_state, zero_grads),
        heads[0],
        tails[0],
        relations[0],
        negatives[0],
        edge_counts[0, 0],
        operator_rows,
    )
    carried_grads = first_pass[4]
    mask_value = partner_mask[0]
    dom_bits = lax.axis_size("dom").bit_length() - 1
    payload = (first_pass[2], first_pass[3])
    payload = relocate(payload, mask_value, list(range(dom_bits)))
    second_pass = train_bucket(
        (first_pass[0], first_pass[1], payload[0], payload[1], carried_grads),
        heads[1],
        tails[1],
        relations[1],
        negatives[1],
        edge_counts[1, 0],
        operator_rows,
    )
    grads = lax.psum_scatter(second_pass[4], ("grp", "dom"), scatter_dimension=0, tiled=True)
    new_acc = operator_state + grads * grads
    new_operators = operators - operator_rate * grads / jnp.sqrt(new_acc)
    return (second_pass[0], second_pass[1], second_pass[2], second_pass[3], new_operators)


def solution(mesh):
    placed = (
        P(("grp", "dom"), None),
        P(("grp", "dom")),
        P(("grp", "dom"), None),
        P(("grp", "dom")),
        P(("grp", "dom"), None),
        P(("grp", "dom"), None),
        P(None, ("grp", "dom")),
        P(None, ("grp", "dom")),
        P(None, ("grp", "dom")),
        P(None, ("grp", "dom"), None),
        P(None, ("grp", "dom")),
        P(),
    )
    return jax.shard_map(
        body,
        mesh=mesh,
        in_specs=placed,
        out_specs=(
            P(("grp", "dom"), None),
            P(("grp", "dom")),
            P(("grp", "dom"), None),
            P(("grp", "dom")),
            P(("grp", "dom"), None),
        ),
        check_vma=False,
    )
```

profile of v0, /device:TPU:2, one launch (start us, length us, event | category | flops | bytes accessed | tf_op | source)
XLA Modules:
  0.0 1932.5 jit_solution(2056289045955717942)
XLA Ops:
  9.4 708.2 %all-gather.3.cloned.1.call-done = f32[256,9,256]{2,1,0:T(8,128)} async-done(((f32[1,9,256]{2,1,0:T(8,128)}), f32[256,9,256]{2,1,0:T(8,128)}) %all-gather.3.cloned.1.call-update) | async-done | bytes 2359312 | tf_op jit(solution)/shard_map/all_gather | solution.py:85
  717.6 4.5 reshape.277
  724.5 352.8 %while.36 = (s32[]{:T(128)}, f32[1024,256]{1,0:T(8,128)S(1)}, f32[1024]{0:T(1024)S(1)}, f32[1024,256]{1,0:T(8,128)S(1)}, f32[1024]{0:T(1024)S(1)}, /*index=5*/f3...) while((s32[]{:T(128)}, f32[1024,256]{1,0:T(8,128)S(1)}, ...), condition=%wide.region_8.9_spmd, body=%wide.region_0.8_spmd.sunk | while | flops 2421178368 | bytes 49136104 | solution.py:57
  742.1 4.3 scatter_custom_fusion.33
  751.4 4.2 scatter_custom_fusion.31
  755.5 4.2 scatter_fusion
  761.8 6.8 scatter_custom_fusion.34
  786.2 4.3 scatter_custom_fusion.33
  791.4 4.0 fusion.95
  795.4 4.2 scatter_custom_fusion.31
  799.6 4.2 scatter_fusion
  805.8 6.8 scatter_custom_fusion.34
  830.3 4.3 scatter_custom_fusion.33
  835.5 4.0 fusion.95
  839.5 4.2 scatter_custom_fusion.31
  843.7 4.2 scatter_fusion
  849.9 6.8 scatter_custom_fusion.34
  874.3 4.3 scatter_custom_fusion.33
  879.6 4.0 fusion.95
  883.6 4.2 scatter_custom_fusion.31
  887.7 4.2 scatter_fusion
  893.9 6.8 scatter_custom_fusion.34
  918.4 4.3 scatter_custom_fusion.33
  923.6 4.0 fusion.95
  927.6 4.2 scatter_custom_fusion.31
  931.8 4.2 scatter_fusion
  938.0 6.8 scatter_custom_fusion.34
  962.5 4.3 scatter_custom_fusion.33
  967.7 4.0 fusion.95
  971.7 4.2 scatter_custom_fusion.31
  975.9 4.2 scatter_fusion
  982.1 6.8 scatter_custom_fusion.34
  1006.5 4.3 scatter_custom_fusion.33
  1011.8 4.0 fusion.95
  1015.7 4.2 scatter_custom_fusion.31
  1019.9 4.2 scatter_fusion
  1026.1 6.8 scatter_custom_fusion.34
  1050.6 4.3 scatter_custom_fusion.33
  1055.8 4.0 fusion.95
  1059.8 4.2 scatter_custom_fusion.31
  1064.0 4.2 scatter_fusion
  1070.2 6.8 scatter_custom_fusion.34
  1078.1 14.1 collective-permute-done
  1092.5 26.4 %collective-permute-done.1 = f32[1024,256]{1,0:T(8,128)S(1)} collective-permute-done((f32[1024,256]{1,0:T(8,128)S(1)}, f32[1024,256]{1,0:T(8,128)S(1)}, u32[]{:S(2)}, u32[]{:S(2)}) %collective-permute-start.1) | collective-permute-done | bytes 1048608 | tf_op jit(solution)/shard_map/ppermute | solution.py:12
  1119.0 41.1 %collective-permute-start.2 = (f32[1024,256]{1,0:T(8,128)S(1)}, f32[1024,256]{1,0:T(8,128)S(1)}, u32[]{:S(2)}, u32[]{:S(2)}) collective-permute-start(f32[1024,256]{1,0:T(8,128)S(1)} %broadcast_select_fusion.1), channel_id=1, source_target_pairs={{0,4},{1,5},{2,6},{3,7},{4,0},{5,1},{6,2},{7,3},{8,12},{9,13},{10,... | collective-permute-start | bytes 3145736 | tf_op jit(solution)/shard_map/ppermute | solution.py:12
  1160.1 46.2 %collective-permute-done.2 = f32[1024,256]{1,0:T(8,128)S(1)} collective-permute-done((f32[1024,256]{1,0:T(8,128)S(1)}, f32[1024,256]{1,0:T(8,128)S(1)}, u32[]{:S(2)}, u32[]{:S(2)}) %collective-permute-start.2) | collective-permute-done | bytes 1048608 | tf_op jit(solution)/shard_map/ppermute | solution.py:12
  1206.5 25.9 %collective-permute-done.3 = f32[1024,256]{1,0:T(8,128)S(1)} collective-permute-done((f32[1024,256]{1,0:T(8,128)S(1)}, f32[1024,256]{1,0:T(8,128)S(1)}, u32[]{:S(2)}, u32[]{:S(2)}) %collective-permute-start.3) | collective-permute-done | bytes 1048608 | tf_op jit(solution)/shard_map/ppermute | solution.py:12
  1232.6 24.0 %collective-permute-start.6 = (f32[1024]{0:T(1024)S(1)}, f32[1024]{0:T(1024)S(1)}, u32[]{:S(2)}, u32[]{:S(2)}) collective-permute-start(f32[1024]{0:T(1024)S(1)} %get-tuple-element.152), channel_id=1, source_target_pairs={{0,1},{1,0},{2,3},{3,2},{4,5},{5,4},{6,7},{7,6},{8,9},{9,8},{10,11... | collective-permute-start | bytes 12296 | tf_op jit(solution)/shard_map/ppermute | solution.py:12
  1258.2 9.8 collective-permute-start.7
  1272.3 4.8 collective-permute-done.8
  1277.4 4.8 collective-permute-done.9
  1282.3 6.4 collective-permute-done.10
  1293.9 88.5 %while.37 = (s32[]{:T(128)}, f32[1024,256]{1,0:T(8,128)S(1)}, f32[1024]{0:T(1024)S(1)}, f32[1024,256]{1,0:T(8,128)S(1)}, f32[1024]{0:T(1024)S(1)}, /*index=5*/f3...) while((s32[]{:T(128)}, f32[1024,256]{1,0:T(8,128)S(1)}, ...), condition=%wide.region_17.18_spmd, body=%wide.region_9.17_spmd.sunk | while | flops 2421178368 | bytes 49136104 | solution.py:57
  1311.8 4.3 scatter_custom_fusion.40
  1317.0 4.0 fusion.111
  1321.0 4.2 scatter_custom_fusion.38
  1325.2 4.2 scatter_fusion.1
  1331.4 6.8 scatter_custom_fusion.41
  1355.8 4.3 scatter_custom_fusion.40
  1361.1 4.0 fusion.111
  1365.1 4.2 scatter_custom_fusion.38
  1369.2 4.2 scatter_fusion.1
  1375.4 6.8 scatter_custom_fusion.41
  1382.6 541.4 %all-reduce.3.cloned.1.call-done = f32[2304,256]{1,0:T(8,128)} async-done(((f32[2304,256]{1,0:T(8,128)}), f32[2304,256]{1,0:T(8,128)}) %all-reduce.3.cloned.1.call-update) | async-done | bytes 2359312
  (428 shorter events, 225.2 us)
Async XLA Ops:
  7.2 710.4 %all-gather.3.cloned.1.call-start = ((), (), s32[]{:S(2)}) async-start(), calls=%async_computation | async-start | bytes 4210688 | tf_op jit(solution)/shard_map/all_gather | solution.py:85
  8.0 1916.1 %all-reduce.3.cloned.1.call-start = ((), (), s32[]{:S(2)}) async-start(), calls=%async_computation.1 | async-start | bytes 4718592
  728.5 3.4 copy-start.8
  731.9 4.4 copy-start.6
  734.1 2.9 copy-start.10
  737.0 3.3 copy-start.12
  737.0 3.3 copy-start.16
  772.6 3.4 copy-start.8
  776.0 4.4 copy-start.6
  781.1 3.3 copy-start.12
  781.1 3.3 copy-start.16
  816.6 3.4 copy-start.8
  820.1 4.4 copy-start.6
  822.2 2.9 copy-start.10
  825.2 3.3 copy-start.12
  825.2 3.3 copy-start.16
  860.7 3.4 copy-start.8
  864.1 4.4 copy-start.6
  866.3 2.9 copy-start.10
  869.2 3.3 copy-start.12
  869.2 3.3 copy-start.16
  904.7 3.4 copy-start.8
  908.2 4.4 copy-start.6
  913.3 3.3 copy-start.12
  913.3 3.3 copy-start.16
  948.8 3.4 copy-start.8
  952.3 4.4 copy-start.6
  957.3 3.3 copy-start.12
  957.4 3.3 copy-start.16
  992.9 3.4 copy-start.8
  996.3 4.4 copy-start.6
  1001.4 3.3 copy-start.12
  1001.4 3.3 copy-start.16
  1036.9 3.4 copy-start.8
  1040.4 4.4 copy-start.6
  1045.5 3.3 copy-start.12
  1045.5 3.3 copy-start.16
  1077.4 14.9 collective-permute-start
  1092.4 26.5 %collective-permute-start.1 = (f32[1024,256]{1,0:T(8,128)S(1)}, f32[1024,256]{1,0:T(8,128)S(1)}, u32[]{:S(2)}, u32[]{:S(2)}) collective-permute-start(f32[1024,256]{1,0:T(8,128)S(1)} %broadcast_select_fusion), channel_id=1, source_target_pairs={{0,2},{1,3},{2,0},{3,1},{4,6},{5,7},{6,4},{7,5},{8,10},{9,11},{10,... | collective-permute-start | bytes 3145736 | tf_op jit(solution)/shard_map/ppermute | solution.py:12
  1119.0 87.3 %collective-permute-start.2 = (f32[1024,256]{1,0:T(8,128)S(1)}, f32[1024,256]{1,0:T(8,128)S(1)}, u32[]{:S(2)}, u32[]{:S(2)}) collective-permute-start(f32[1024,256]{1,0:T(8,128)S(1)} %broadcast_select_fusion.1), channel_id=1, source_target_pairs={{0,4},{1,5},{2,6},{3,7},{4,0},{5,1},{6,2},{7,3},{8,12},{9,13},{10,... | collective-permute-start | bytes 3145736 | tf_op jit(solution)/shard_map/ppermute | solution.py:12
  1206.4 26.0 %collective-permute-start.3 = (f32[1024,256]{1,0:T(8,128)S(1)}, f32[1024,256]{1,0:T(8,128)S(1)}, u32[]{:S(2)}, u32[]{:S(2)}) collective-permute-start(f32[1024,256]{1,0:T(8,128)S(1)} %broadcast_select_fusion.2), channel_id=1, source_target_pairs={{0,8},{1,9},{2,10},{3,11},{4,12},{5,13},{6,14},{7,15},{8,0},{9,1},... | collective-permute-start | bytes 3145736 | tf_op jit(solution)/shard_map/ppermute | solution.py:12
  1232.5 35.5 %collective-permute-start.4 = (f32[1024,256]{1,0:T(8,128)S(1)}, f32[1024,256]{1,0:T(8,128)S(1)}, u32[]{:S(2)}, u32[]{:S(2)}) collective-permute-start(f32[1024,256]{1,0:T(8,128)S(1)} %broadcast_select_fusion.3), channel_id=1, source_target_pairs={{0,16},{1,17},{2,18},{3,19},{4,20},{5,21},{6,22},{7,23},{8,24},{9,... | collective-permute-start | bytes 3145736 | tf_op jit(solution)/shard_map/ppermute | solution.py:12
  1232.6 25.6 %collective-permute-start.6 = (f32[1024]{0:T(1024)S(1)}, f32[1024]{0:T(1024)S(1)}, u32[]{:S(2)}, u32[]{:S(2)}) collective-permute-start(f32[1024]{0:T(1024)S(1)} %get-tuple-element.152), channel_id=1, source_target_pairs={{0,1},{1,0},{2,3},{3,2},{4,5},{5,4},{6,7},{7,6},{8,9},{9,8},{10,11... | collective-permute-start | bytes 12296 | tf_op jit(solution)/shard_map/ppermute | solution.py:12
  1258.2 11.4 collective-permute-start.7
  1268.1 25.7 %collective-permute-start.5 = (f32[1024,256]{1,0:T(8,128)S(1)}, f32[1024,256]{1,0:T(8,128)}, u32[]{:S(2)}, u32[]{:S(2)}) collective-permute-start(f32[1024,256]{1,0:T(8,128)S(1)} %broadcast_select_fusion.4), channel_id=1, source_target_pairs={{0,32},{1,33},{2,34},{3,35},{4,36},{5,37},{6,38},{7,39},{8,40},{9,... | collective-permute-start | bytes 3145736 | tf_op jit(solution)/shard_map/ppermute | solution.py:12
  1269.6 7.5 collective-permute-start.8
  1277.1 5.1 collective-permute-start.9
  1282.2 6.5 collective-permute-start.10
  1288.7 5.1 collective-permute-start.11
  1298.1 3.4 copy-start.9
  1301.6 4.4 copy-start.7
  1306.7 3.3 copy-start.13
  1306.7 3.3 copy-start.17
  1342.2 3.4 copy-start.9
  1345.6 4.4 copy-start.7
  1347.8 2.9 copy-start.11
  1350.7 3.3 copy-start.13
  1350.7 3.3 copy-start.17
  1382.5 542.9 %copy-start = (f32[1024,256]{1,0:T(8,128)}, f32[1024,256]{1,0:T(8,128)S(1)}, u32[]{:S(2)}) copy-start(f32[1024,256]{1,0:T(8,128)S(1)} %get-tuple-element.144) | copy-start | bytes 3145732
  1382.5 542.9 %copy-start.3 = (f32[1024,256]{1,0:T(8,128)}, f32[1024,256]{1,0:T(8,128)S(1)}, u32[]{:S(2)}) copy-start(f32[1024,256]{1,0:T(8,128)S(1)} %get-tuple-element.146) | copy-start | bytes 3145732
  1382.5 542.9 %copy-start.18 = (f32[1024]{0:T(1024)}, f32[1024]{0:T(1024)S(1)}, u32[]{:S(2)}) copy-start(f32[1024]{0:T(1024)S(1)} %get-tuple-element.145) | copy-start | bytes 12292
  1382.5 542.9 %copy-start.21 = (f32[1024]{0:T(1024)}, f32[1024]{0:T(1024)S(1)}, u32[]{:S(2)}) copy-start(f32[1024]{0:T(1024)S(1)} %get-tuple-element.147) | copy-start | bytes 12292
  1382.5 541.5 %copy-start.22 = (f32[9,256]{1,0:T(8,128)S(1)}, f32[9,256]{1,0:T(8,128)}, u32[]{:S(2)}) copy-start(f32[9,256]{1,0:T(8,128)} %param.20) | copy-start | bytes 27652
  1382.5 541.5 %copy-start.27 = (f32[9,256]{1,0:T(8,128)S(1)}, f32[9,256]{1,0:T(8,128)}, u32[]{:S(2)}) copy-start(f32[9,256]{1,0:T(8,128)} %param.21) | copy-start | bytes 27652
  (35 other events, 55.1 us)
Sparse Core Ops, SparseCore 0:
  9.9 707.6 all-gather.2
  1382.7 541.2 all-reduce.2
where the time goes:
time: 1930 us
  waiting for transfers between devices  1380 us (72%)
  other arithmetic  256 us (13%)
  local copies, waits for them, and re-layouts  112 us (6%)
  starting transfers between devices  81.2 us (4%)
  matrix products  80.8 us (4%)
    all_gather x1, waiting for transfers between devices, body(): lax.all_gather(operators, ('grp', 'dom'), axis=0, tiled=True)  708 us
    unnamed x3, waiting for transfers between devices  542 us
    ppermute x12, waiting for transfers between devices, swapped(): lax.ppermute(x, axis, [(i, i ^ 1 << distance) for i in range(lax.axis_siz...  133 us
    scatter-add x20, other arithmetic, block_update(): jnp.zeros_like(right_part).at[tail_index].add(tail_side).at[neg_index]  83.9 us
    ppermute x12, starting transfers between devices, swapped(): lax.ppermute(x, axis, [(i, i ^ 1 << distance) for i in range(lax.axis_siz...  81.1 us
    scatter-add x10, other arithmetic, block_update(): rel_grads = rel_grads.at[rel_index].add(head_side * head_rows)  68.3 us
    scatter-add x10, other arithmetic, block_update(): jnp.zeros_like(left_part).at[head_index].add(head_side * diag_rows)  42.6 us
    dot_general x10, matrix products, block_update(): jnp.einsum('cn,cd->nd', neg_grad, scaled_heads, precision=highest)  39.9 us
  transfers between devices with their start and end apart: 14, of which 12 were waited for; matrix products, arithmetic and copies ran while one was open for 0% of the time, Pallas kernels for 0%

commit v1 on v0

v1 whole, which is shorter than its diff:
```python
import jax
import jax.numpy as jnp
from jax import lax
from jax.experimental import pallas as pl
from jax.experimental.pallas import tpu as pltpu
from jax.sharding import PartitionSpec as P

D = 256
PART = 1024
SPAN = 512
REL = 2304
VMEM = pl.BlockSpec(memory_space=pltpu.VMEM)
SMEM = pl.BlockSpec(memory_space=pltpu.SMEM)
AXES = ("grp", "dom")
STAGES = ((1, 2, 3, 4, 5, 6, 7), (16, 32, 48), (8, 128, 136), (64,))


def split(x):
    high = x.astype(jnp.bfloat16)
    return high, (x - high.astype(jnp.float32)).astype(jnp.bfloat16)


def mm(x, y):
    return jnp.dot(x, y, preferred_element_type=jnp.float32)


def mm_nt(x, y):
    return lax.dot_general(x, y, (((1,), (1,)), ((), ())), preferred_element_type=jnp.float32)


def block_turns(count_ref):
    return (count_ref[0] + SPAN - 1) // SPAN


def one_hot(rows, index_row, base=0):
    ids = base + lax.broadcasted_iota(jnp.int32, (rows, SPAN), 0)
    return jnp.where(ids == index_row, 1.0, 0.0).astype(jnp.bfloat16)


def gather_kernel(count_ref, rel_ref, ops_ref, w_ref, hot, ops_split):
    ops_t = ops_ref[...].T
    high, low = split(ops_t)
    ops_split[0:D] = high
    ops_split[D : 2 * D] = low

    def one(k, _):
        index_row = rel_ref[pl.ds(k, 1), :]
        for c in range(REL // 256):
            hot[c * 256 : (c + 1) * 256] = one_hot(256, index_row, c * 256)
        both = mm(ops_split[...], hot[...])
        w_ref[k] = both[:D] + both[D:]
        return 0

    lax.fori_loop(0, block_turns(count_ref), one, 0)


def grads_kernel(count1_ref, count2_ref, rel1_ref, rel2_ref, z1_ref, z2_ref, g_ref, hot, acc):
    acc[...] = jnp.zeros_like(acc)

    def scatter(rel_ref, z_ref, turns):
        def one(k, _):
            index_row = rel_ref[pl.ds(k, 1), :]
            for c in range(REL // 256):
                rows = slice(c * 256, (c + 1) * 256)
                hot[rows] = one_hot(256, index_row, c * 256)
            acc[...] += mm_nt(hot[...], z_ref[k])
            return 0

        lax.fori_loop(0, turns, one, 0)

    scatter(rel1_ref, z1_ref, block_turns(count1_ref))
    scatter(rel2_ref, z2_ref, block_turns(count2_ref))
    g_ref[...] = acc[:, :D] + acc[:, D:]


def train_kernel(second, count_ref, heads_ref, tails_ref, negs_ref, w_ref, l_ref, ls_ref, r_ref, rs_ref,
                 l_out, ls_out, r_out, rs_out, z_ref,
                 lt, rt, l_split, r_split, r_cols, hot, s3, cat, score, c_high, c_low):
    def set_left(value):
        lt[...] = value
        high, low = split(value)
        l_split[0:D] = high
        l_split[D : 2 * D] = low

    def set_right(value):
        rt[...] = value
        high, low = split(value)
        r_split[0:D] = high
        r_split[D : 2 * D] = low
        across = value.T
        high, low = split(across)
        r_cols[:, 0:D] = high
        r_cols[:, D : 2 * D] = high
        r_cols[:, 2 * D : 3 * D] = low

    if second:
        set_left(l_ref[...])
        set_right(r_ref[0:D, :])
        rs_out[...] = r_ref[D : D + 1, :]
    else:
        set_left(l_ref[...].T)
        set_right(r_ref[...].T)
        rs_out[...] = rs_ref[...]
    ls_out[...] = ls_ref[...]
    count = count_ref[0]

    def one(k, _):
        head_row = heads_ref[pl.ds(k, 1), :]
        tail_row = tails_ref[pl.ds(k, 1), :]
        neg_row = negs_ref[pl.ds(k, 1), :]
        slots = k * SPAN + lax.broadcasted_iota(jnp.int32, (1, SPAN), 1)
        live = jnp.where(slots < count, 1.0, 0.0)
        half = live * (0.5 / SPAN)
        for c in range(8):
            hot[c * 128 : (c + 1) * 128] = one_hot(128, head_row, c * 128)
        w_t = w_ref[k]
        both = mm(l_split[...], hot[...])
        h_t = both[:D] + both[D:]
        s_high, s_low = split(h_t * w_t)
        s3[0:D] = s_high
        s3[D : 2 * D] = s_low
        s3[2 * D : 3 * D] = s_high
        score[...] = mm(r_cols[...], s3[...])
        positive = jnp.zeros((8, SPAN), jnp.float32)
        for c in range(PART // 32):
            rows = slice(c * 32, (c + 1) * 32)
            ids = c * 32 + lax.broadcasted_iota(jnp.int32, (32, SPAN), 0)
            a = score[rows]
            times = jnp.sum(jnp.where(ids == neg_row, 1.0, 0.0), axis=1, keepdims=True)
            picked = jnp.where(ids == tail_row, a, 0.0)
            positive = positive + (picked[0:8] + picked[8:16]) + (picked[16:24] + picked[24:32])
            score[rows] = (jnp.tanh(0.5 * a) + 1.0) * times * half
        positive = jnp.sum(positive, axis=0, keepdims=True)
        pos_grad = -jax.nn.sigmoid(-positive) * live
        for c in range(PART // 32):
            rows = slice(c * 32, (c + 1) * 32)
            ids = c * 32 + lax.broadcasted_iota(jnp.int32, (32, SPAN), 0)
            high, low = split(score[rows] + jnp.where(ids == tail_row, pos_grad, 0.0))
            c_high[rows] = high
            c_low[rows] = low
        both = mm(r_split[...], c_high[...])
        q_t = both[:D] + both[D:] + mm(r_split[0:D], c_low[...])
        high, low = split(q_t * h_t)
        z_ref[k, 0:D] = high
        z_ref[k, D : 2 * D] = low
        high, low = split(q_t * w_t)
        cat[0:D] = high
        cat[D : 2 * D] = low
        both = mm_nt(cat[...], hot[...])
        grad = both[:D] + both[D:]
        acc = ls_out[...] + jnp.mean(grad * grad, axis=0, keepdims=True)
        ls_out[...] = acc
        set_left(lt[...] - grad * (0.1 * lax.rsqrt(acc)))
        both = mm_nt(s3[0 : 2 * D], c_high[...])
        grad = both[:D] + both[D:] + mm_nt(s3[0:D], c_low[...])
        acc = rs_out[...] + jnp.mean(grad * grad, axis=0, keepdims=True)
        rs_out[...] = acc
        set_right(rt[...] - grad * (0.1 * lax.rsqrt(acc)))
        return 0

    lax.fori_loop(0, block_turns(count_ref), one, 0)
    if second:
        l_out[...] = lt[...].T
        r_out[...] = rt[...].T
    else:
        l_out[...] = lt[...]
        r_out[0:D, :] = rt[...]
        r_out[D : D + 8, :] = jnp.broadcast_to(rs_out[...], (8, PART))


def params():
    return pltpu.CompilerParams(vmem_limit_bytes=56 * 1024 * 1024)


def gather_rows(count, rel, ops):
    return pl.pallas_call(
        gather_kernel,
        out_shape=jax.ShapeDtypeStruct((8, D, SPAN), jnp.float32),
        in_specs=[SMEM, VMEM, VMEM],
        out_specs=VMEM,
        scratch_shapes=[pltpu.VMEM((REL, SPAN), jnp.bfloat16), pltpu.VMEM((2 * D, REL), jnp.bfloat16)],
        compiler_params=params(),
        cost_estimate=pl.CostEstimate(flops=8 * 4 * REL * SPAN * D, bytes_accessed=6 * 2**20, transcendentals=0),
        name="gather_operators",
    )(count, rel, ops)


def relation_grads(count1, count2, rel1, rel2, z1, z2):
    return pl.pallas_call(
        grads_kernel,
        out_shape=jax.ShapeDtypeStruct((REL, D), jnp.float32),
        in_specs=[SMEM, SMEM, VMEM, VMEM, VMEM, VMEM],
        out_specs=VMEM,
        scratch_shapes=[pltpu.VMEM((REL, SPAN), jnp.bfloat16), pltpu.VMEM((REL, 2 * D), jnp.float32)],
        compiler_params=params(),
        name="relation_grads",
    )(count1, count2, rel1, rel2, z1, z2)


def train(second, count, heads, tails, negs, w, left, left_state, right, right_state):
    f32, bf16 = jnp.float32, jnp.bfloat16
    if second:
        shapes = [((PART, D), f32), ((1, PART), f32), ((PART, D), f32), ((1, PART), f32)]
    else:
        shapes = [((D, PART), f32), ((1, PART), f32), ((D + 8, PART), f32), ((1, PART), f32)]
    shapes.append(((8, 2 * D, SPAN), bf16))
    return pl.pallas_call(
        lambda *refs: train_kernel(second, *refs),
        out_shape=[jax.ShapeDtypeStruct(*s) for s in shapes],
        in_specs=[SMEM] + [VMEM] * 8,
        out_specs=[VMEM] * 5,
        scratch_shapes=[
            pltpu.VMEM((D, PART), f32),
            pltpu.VMEM((D, PART), f32),
            pltpu.VMEM((2 * D, PART), bf16),
            pltpu.VMEM((2 * D, PART), bf16),
            pltpu.VMEM((PART, 3 * D), bf16),
            pltpu.VMEM((PART, SPAN), bf16),
            pltpu.VMEM((3 * D, SPAN), bf16),
            pltpu.VMEM((2 * D, SPAN), bf16),
            pltpu.VMEM((PART, SPAN), f32),
            pltpu.VMEM((PART, SPAN), bf16),
            pltpu.VMEM((PART, SPAN), bf16),
        ],
        compiler_params=params(),
        name="train_second" if second else "train_first",
    )(count, heads, tails, negs, w, left, left_state, right, right_state)


def exchange(x, mask):
    return lax.ppermute(x, AXES, [(i, i ^ mask) for i in range(256)])


def gather_all(x):
    x = x.reshape(1, 18, 128)
    for masks in STAGES:
        x = jnp.concatenate([x] + [exchange(x, m) for m in masks], axis=0)
    return x.reshape(REL, D)


def scatter_sum(g):
    g = g.reshape(256, 18, 128)
    for masks in STAGES[::-1]:
        n = g.shape[0] // (len(masks) + 1)
        total = g[:n]
        for j, m in enumerate(masks):
            total = total + exchange(g[(j + 1) * n : (j + 2) * n], m)
        g = total
    return g.reshape(9, D)


def row_positions(relations):
    me = lax.axis_index(AXES)
    owner = relations * 7282 >> 16
    away = owner ^ me
    place = (
        (away & 7)
        | (away >> 4 & 3) << 3
        | (away >> 3 & 1) << 5
        | (away >> 7 & 1) << 6
        | (away >> 6 & 1) << 7
    )
    return place * 9 + (relations - owner * 9)


def move(right, mask):
    branches = [
        (lambda x, m=m: lax.ppermute(x, "dom", [(i, i ^ m) for i in range(64)])) for m in range(1, 64)
    ]
    return lax.switch(mask - 1, branches, right)


def body(left_table, left_state, right_table, right_state, operators, operator_state,
         heads, tails, relations, negatives, edge_counts, partner_mask):
    ops = gather_all(operators)
    rel = row_positions(relations).reshape(2, 8, SPAN)
    heads = heads.reshape(2, 8, SPAN)
    tails = tails.reshape(2, 8, SPAN)
    w1 = gather_rows(edge_counts[0], rel[0], ops)
    left, ls, right, _, z1 = train(
        False, edge_counts[0], heads[0], tails[0], negatives[0], w1,
        left_table, left_state.reshape(1, PART), right_table, right_state.reshape(1, PART),
    )
    w2 = gather_rows(edge_counts[1], rel[1], ops)
    right = move(right, partner_mask[0])
    left, ls, right, rs, z2 = train(
        True, edge_counts[1], heads[1], tails[1], negatives[1], w2, left, ls, right, ls
    )
    grads = scatter_sum(relation_grads(edge_counts[0], edge_counts[1], rel[0], rel[1], z1, z2))
    new_acc = operator_state + grads * grads
    new_operators = operators - 0.5 * grads / jnp.sqrt(new_acc)
    return left, ls.reshape(PART), right, rs.reshape(PART), new_operators


def solution(mesh):
    whole = P(AXES)
    placed = (
        P(AXES, None), whole, P(AXES, None), whole, P(AXES, None), P(AXES, None),
        P(None, AXES), P(None, AXES), P(None, AXES), P(None, AXES, None), P(None, AXES), P(),
    )
    return jax.shard_map(
        body,
        mesh=mesh,
        in_specs=placed,
        out_specs=(P(AXES, None), whole, P(AXES, None), whole, P(AXES, None)),
        check_vma=False,
    )
```

time: 1930 us -> 373 us (0.19)
  waiting for transfers between devices: 1380 us -> 99.6 us
  other arithmetic: 256 us -> 2.84 us
  local copies, waits for them, and re-layouts: 112 us -> 27 us
  matrix products: 80.8 us -> 0 us
  starting transfers between devices: 81.2 us -> 160 us
  Pallas kernels: 0 us -> 64.3 us
    all_gather x1 -> x0, waiting for transfers between devices: 708 us -> none  [body(): lax.all_gather(operators, ('grp', 'dom'), axis=0, tiled=True)]
    unnamed x3 -> x0, waiting for transfers between devices: 542 us -> none
    scatter-add x40 -> x0, other arithmetic: 195 us -> none  [the longest x20 83.9 us: block_update(): jnp.zeros_like(right_part).at[tail_index].add(tail_side).at[neg_index]]
    gather x40 -> x0, local copies, waits for them, and re-layouts: 93.8 us -> none  [the longest x10 33.3 us: block_update(): diag_rows = operator_rows[rel_index]]
    dot_general x30 -> x0, matrix products: 80.8 us -> none  [the longest x10 39.9 us: block_update(): jnp.einsum('cn,cd->nd', neg_grad, scaled_heads, precision=highest)]
    ppermute x12 -> x29, starting transfers between devices: 81.1 us -> 160 us  [the longest x28 95.3 us: exchange(): return lax.ppermute(x, AXES, [(i, i ^ mask) for i in range(256)])]
    pallas_call x0 -> x5, Pallas kernels: none -> 64.3 us  [the longest x2 35.9 us: train(): pl.pallas_call(lambda *refs: train_kernel(second, *refs), out_shape=[jax....]
    ppermute x12 -> x29, waiting for transfers between devices: 133 us -> 99.6 us  [the longest x28 52.7 us: exchange(): return lax.ppermute(x, AXES, [(i, i ^ mask) for i in range(256)])]
  transfers between devices with their start and end apart: 14 -> 29, of which waited for: 12 -> 16; matrix products, arithmetic and copies ran while one was open for 0% -> 2% of each run, Pallas kernels for 0% -> 0%
where the time goes in v1:
time: 373 us; the launch traced here: 374 us
  starting transfers between devices  160 us (43%)
  waiting for transfers between devices  99.6 us (27%)
  Pallas kernels  64.3 us (17%)
  local copies, waits for them, and re-layouts  27 us (7%)
  loops' own time  18.4 us (5%)
    ppermute x28, starting transfers between devices, exchange(): return lax.ppermute(x, AXES, [(i, i ^ mask) for i in range(256)])  95.3 us
    ppermute x1, starting transfers between devices, move(): lax.ppermute(x, 'dom', [(i, i ^ m) for i in range(64)])  64.4 us
    ppermute x28, waiting for transfers between devices, exchange(): return lax.ppermute(x, AXES, [(i, i ^ mask) for i in range(256)])  52.7 us
    ppermute x1, waiting for transfers between devices, move(): lax.ppermute(x, 'dom', [(i, i ^ m) for i in range(64)])  46.9 us
    pallas_call x2, Pallas kernels, train(): pl.pallas_call(lambda *refs: train_kernel(second, *refs), out_shape=[jax....  35.9 us
    another operation x1, loops' own time, move(): return lax.switch(mask - 1, branches, right)  18.4 us
    pallas_call x2, Pallas kernels, gather_rows(): pl.pallas_call(gather_kernel, out_shape=jax.ShapeDtypeStruct((8, D, SPAN)...  16 us
    concatenate x4, local copies, waits for them, and re-layouts, gather_all(): x = jnp.concatenate([x] + [exchange(x, m) for m in masks], axis=0)  13.2 us
  transfers between devices with their start and end apart: 29, of which 16 were waited for; matrix products, arithmetic and copies ran while one was open for 2% of the time, Pallas kernels for 0%

profile of v1, /device:TPU:2, one launch (start us, length us, event | category | flops | bytes accessed | tf_op | source)
XLA Modules:
  0.0 373.8 jit_solution(1193371468251762030)
XLA Ops:
  0.6 0.7 reshape.55
  1.4 5.9 %collective-permute-start.69 = (f32[1,18,128]{2,1,0:T(8,128)S(1)}, f32[1,18,128]{2,1,0:T(8,128)S(1)}, u32[]{:S(2)}, u32[]{:S(2)}) collective-permute-start(f32[1,18,128]{2,1,0:T(8,128)S(1)} %reshape.55), channel_id=1, source_target_pairs={{0,7},{1,6},{2,5},{3,4},{4,3},{5,2},{6,1},{7,0},{8,15},{9,14},{10,... | collective-permute-start | bytes 27656 | tf_op jit(solution)/shard_map/ppermute | solution.py:231
  7.2 0.4 collective-permute-start.68
  7.7 4.1 %collective-permute-start.67 = (f32[1,18,128]{2,1,0:T(8,128)S(1)}, f32[1,18,128]{2,1,0:T(8,128)S(1)}, u32[]{:S(2)}, u32[]{:S(2)}) collective-permute-start(f32[1,18,128]{2,1,0:T(8,128)S(1)} %reshape.55), channel_id=1, source_target_pairs={{0,5},{1,4},{2,7},{3,6},{4,1},{5,0},{6,3},{7,2},{8,13},{9,12},{10,... | collective-permute-start | bytes 27656 | tf_op jit(solution)/shard_map/ppermute | solution.py:231
  11.8 1.8 collective-permute-start.66
  13.6 0.6 collective-permute-start.63
  14.2 3.1 collective-permute-done.63
  17.3 1.1 collective-permute-start.64
  18.4 3.6 collective-permute-done.64
  22.0 1.8 collective-permute-start.65
  23.8 3.7 collective-permute-done.65
  27.6 0.6 collective-permute-start.70
  28.2 2.2 collective-permute-start.72
  30.4 1.4 collective-permute-start.71
  31.8 0.5 collective-permute-done.70
  32.3 4.2 %collective-permute-done.71 = f32[8,18,128]{2,1,0:T(8,128)S(1)} collective-permute-done((f32[8,18,128]{2,1,0:T(8,128)S(1)}, f32[8,18,128]{2,1,0:T(8,128)S(1)}, u32[]{:S(2)}, u32[]{:S(2)}) %collective-permute-start.71) | collective-permute-done | bytes 73760 | tf_op jit(solution)/shard_map/ppermute | solution.py:231
  36.5 3.3 collective-permute-start.73
  39.8 0.7 collective-permute-start.74
  40.5 0.4 collective-permute-start.75
  41.6 6.0 %collective-permute-done.73 = f32[32,18,128]{2,1,0:T(8,128)S(1)} collective-permute-done((f32[32,18,128]{2,1,0:T(8,128)S(1)}, f32[32,18,128]{2,1,0:T(8,128)S(1)}, u32[]{:S(2)}, u32[]{:S(2)}) %collective-permute-start.73) | collective-permute-done | bytes 294944 | tf_op jit(solution)/shard_map/ppermute | solution.py:231
  47.6 4.5 %collective-permute-done.74 = f32[32,18,128]{2,1,0:T(8,128)S(1)} collective-permute-done((f32[32,18,128]{2,1,0:T(8,128)S(1)}, f32[32,18,128]{2,1,0:T(8,128)S(1)}, u32[]{:S(2)}, u32[]{:S(2)}) %collective-permute-start.74) | collective-permute-done | bytes 294944 | tf_op jit(solution)/shard_map/ppermute | solution.py:231
  52.3 1.2 copy.17
  53.8 0.6 squeeze.46.rel_ref.rel1_ref
  54.4 0.6 squeeze.41.rel_ref.rel2_ref
  55.0 0.6 squeeze.39.refs_2_
  55.6 0.6 squeeze.44.refs_2_
  56.3 0.6 squeeze.43.refs_1_
  56.9 0.6 squeeze.38.refs_1_
  57.5 0.6 fusion.19
  58.1 0.6 slice_bitcast_fusion
  59.1 8.9 %concatenate.18 = f32[256,18,128]{2,0,1:T(8,128)} concatenate(f32[1,18,128]{2,0,1:T(1,128)S(1)} %copy.18, f32[1,18,128]{2,0,1:T(1,128)S(1)} %copy.19, f32[1,18,128]{2,0,1:T(1,128)S(1)} %copy.20, f32[1,18,128]{2,0,1:T(1,128)S(1)} %copy.21, f32[1,18,128]{2,0,1:T(1,128)S(1)} %copy.22, f32[1,18,128]{2,0,1:T(1,128)S(1)} %copy.23, f32[1,18,128]{2,0,1:T(1,128)S(1)} %copy.24, ...), dimensions={0} | concatenate | bytes 4718592 | tf_op jit(solution)/shard_map/concatenate | solution.py:237
  68.0 3.1 copy.32
  71.1 1.8 reshape.56.ops_ref
  72.8 6.9 %gather_operators.3.refs_4_ = f32[8,256,512]{2,1,0:T(8,128)} custom-call(s32[1]{0:T(128)} %bitcast.2.count_ref.refs_0_.count1_ref, s32[8,512]{1,0:T(8,128)} %squeeze.46.rel_ref.rel1_ref, f32[2304,256]{1,0:T(8,128)} %reshape.56.ops_ref), custom_call_target="tpu_custom_call" | custom-call | flops 9663676416 | bytes 6291456 | tf_op jit(solution)/shard_map/gather_operators/pallas_call | solution.py:176
  79.8 9.1 %gather_operators.2.refs_4_ = f32[8,256,512]{2,1,0:T(8,128)} custom-call(s32[1]{0:T(128)} %bitcast.count_ref.refs_0_.count2_ref, s32[8,512]{1,0:T(8,128)} %squeeze.41.rel_ref.rel2_ref, f32[2304,256]{1,0:T(8,128)} %reshape.56.ops_ref), custom_call_target="tpu_custom_call" | custom-call | flops 9663676416 | bytes 6291456 | tf_op jit(solution)/shard_map/gather_operators/pallas_call | solution.py:176
  88.8 12.3 %train_first.1 = (f32[256,1024]{1,0:T(8,128)}, f32[1,1024]{1,0:T(1,128)}, f32[264,1024]{1,0:T(8,128)S(1)}, f32[1,1024]{1,0:T(1,128)}, bf16[8,512,512]{2,1,0:T(8,128)(2,1)}) custom-call(s32[1]{0:T(128)} %bitcast.2.count_ref.refs_0_.count1_ref, s32[8,512]{1,0:T(8,128)} %squeeze.43.refs_1_, s32[8,512]{1,0:T(8,128)} %squeeze.44.refs_2_, ...), custom_call_target="tpu_custom_call" | custom-call | tf_op jit(solution)/shard_map/train_first/pallas_call | solution.py:207
  101.1 129.7 %conditional.1 = (f32[264,1024]{1,0:T(8,128)}) conditional(s32[]{:T(128)} %bitcast.6, f32[264,1024]{1,0:T(8,128)S(1)} %get-tuple-element.143, f32[264,1024]{1,0:T(8,128)S(1)} %get-tuple-element.143, f32[264,1024]{1,0:T(8,128)S(1)} %get-tuple-element.143, f32[264,1024]{1,0:T(8,128)S(1)} %get-tuple-element.143, ...), branch_computations={%region_0.0_spmd, %region_1.0_spmd, %region_2.0_spmd, %region_3.0_... | conditional | bytes 4325424 | solution.py:270
  110.5 64.4 %collective-permute-start.53 = (f32[264,1024]{1,0:T(8,128)S(1)}, f32[264,1024]{1,0:T(8,128)}, u32[]{:S(2)}, u32[]{:S(2)}) collective-permute-start(f32[264,1024]{1,0:T(8,128)S(1)} %param.53), channel_id=1, source_target_pairs={{0,54},{1,55},{2,52},{3,53},{4,50},{5,51},{6,48},{7,49},{8,62},{9,... | collective-permute-start | bytes 3244040 | tf_op jit(solution)/shard_map/cond/branch_53_fun/ppermute | solution.py:268
  174.9 46.9 %collective-permute-done.53 = f32[264,1024]{1,0:T(8,128)} collective-permute-done((f32[264,1024]{1,0:T(8,128)S(1)}, f32[264,1024]{1,0:T(8,128)}, u32[]{:S(2)}, u32[]{:S(2)}) %collective-permute-start.53) | collective-permute-done | bytes 1081376 | tf_op jit(solution)/shard_map/cond/branch_53_fun/ppermute | solution.py:268
  230.8 23.6 %train_second.1 = (f32[1024,256]{1,0:T(8,128)}, f32[1,1024]{1,0:T(1,128)}, f32[1024,256]{1,0:T(8,128)}, f32[1,1024]{1,0:T(1,128)}, bf16[8,512,512]{2,1,0:T(8,128)(2,1)}) custom-call(s32[1]{0:T(128)} %bitcast.count_ref.refs_0_.count2_ref, s32[8,512]{1,0:T(8,128)} %squeeze.38.refs_1_, s32[8,512]{1,0:T(8,128)} %squeeze.39.refs_2_, ...), custom_call_target="tpu_custom_call" | custom-call | tf_op jit(solution)/shard_map/train_second/pallas_call | solution.py:207
  254.4 12.4 %relation_grads.1 = f32[2304,256]{1,0:T(8,128)} custom-call(s32[1]{0:T(128)} %bitcast.2.count_ref.refs_0_.count1_ref, s32[1]{0:T(128)} %bitcast.count_ref.refs_0_.count2_ref, s32[8,512]{1,0:T(8,128)} %squeeze.46.rel_ref.rel1_ref, s32[8,512]{1,0:T(8,128)} %squeeze.41.rel_ref.rel2_ref, bf16[8,512,512]{2,1,0:T(8,128)(2,1)} %get-tuple-element.148.z1_ref, ...), custom_call_target="tpu_custom_call" | custom-call | tf_op jit(solution)/shard_map/relation_grads/pallas_call | solution.py:189
  266.8 2.8 fusion.15
  269.6 1.4 slice.115
  271.0 1.2 copy.33
  272.3 1.2 collective-permute-start.77
  273.6 2.7 collective-permute-done.77
  276.3 2.0 copy_add_fusion
  278.4 11.6 %collective-permute-start.78 = (f32[32,18,128]{2,1,0:T(8,128)S(1)}, f32[32,18,128]{2,1,0:T(8,128)S(1)}, u32[]{:S(2)}, u32[]{:S(2)}) collective-permute-start(f32[32,18,128]{2,1,0:T(8,128)S(1)} %get-tuple-element.160), channel_id=1, source_target_pairs={{0,8},{1,9},{2,10},{3,11},{4,12},{5,13},{6,14},{7,15},{8,0},{9,1},... | collective-permute-start | bytes 884744 | tf_op jit(solution)/shard_map/ppermute | solution.py:231
  290.0 23.8 %collective-permute-start.80 = (f32[32,18,128]{2,1,0:T(8,128)S(1)}, f32[32,18,128]{2,1,0:T(8,128)S(1)}, u32[]{:S(2)}, u32[]{:S(2)}) collective-permute-start(f32[32,18,128]{2,1,0:T(8,128)S(1)} %get-tuple-element.161), channel_id=1, source_target_pairs={{0,136},{1,137},{2,138},{3,139},{4,140},{5,141},{6,142},{7,143},{8... | collective-permute-start | bytes 884744 | tf_op jit(solution)/shard_map/ppermute | solution.py:231
  313.8 14.2 %collective-permute-done.80 = f32[32,18,128]{2,1,0:T(8,128)S(1)} collective-permute-done((f32[32,18,128]{2,1,0:T(8,128)S(1)}, f32[32,18,128]{2,1,0:T(8,128)S(1)}, u32[]{:S(2)}, u32[]{:S(2)}) %collective-permute-start.80) | collective-permute-done | bytes 294944 | tf_op jit(solution)/shard_map/ppermute | solution.py:231
  328.0 1.1 collective-permute-done.79
  329.2 15.4 %collective-permute-start.81 = (f32[8,18,128]{2,1,0:T(8,128)S(1)}, f32[8,18,128]{2,1,0:T(8,128)S(1)}, u32[]{:S(2)}, u32[]{:S(2)}) collective-permute-start(f32[8,18,128]{2,1,0:T(8,128)S(1)} %get-tuple-element.163), channel_id=1, source_target_pairs={{0,16},{1,17},{2,18},{3,19},{4,20},{5,21},{6,22},{7,23},{8,24},{9,... | collective-permute-start | bytes 221192 | tf_op jit(solution)/shard_map/ppermute | solution.py:231
  344.6 0.5 collective-permute-start.83
  345.1 1.7 collective-permute-start.82
  346.8 0.8 collective-permute-done.81
  347.6 2.2 collective-permute-done.83
  349.8 1.6 collective-permute-done.82
  351.4 4.0 %collective-permute-start.84 = (f32[1,18,128]{2,1,0:T(8,128)S(1)}, f32[1,18,128]{2,1,0:T(8,128)S(1)}, u32[]{:S(2)}, u32[]{:S(2)}) collective-permute-start(f32[1,18,128]{2,1,0:T(8,128)S(1)} %get-tuple-element.166), channel_id=1, source_target_pairs={{0,1},{1,0},{2,3},{3,2},{4,5},{5,4},{6,7},{7,6},{8,9},{9,8},{10,11... | collective-permute-start | bytes 27656 | tf_op jit(solution)/shard_map/ppermute | solution.py:231
  355.4 3.7 collective-permute-start.90
  359.1 5.8 %collective-permute-start.88 = (f32[1,18,128]{2,1,0:T(8,128)S(1)}, f32[1,18,128]{2,1,0:T(8,128)S(1)}, u32[]{:S(2)}, u32[]{:S(2)}) collective-permute-start(f32[1,18,128]{2,1,0:T(8,128)S(1)} %get-tuple-element.169), channel_id=1, source_target_pairs={{0,5},{1,4},{2,7},{3,6},{4,1},{5,0},{6,3},{7,2},{8,13},{9,12},{10,... | collective-permute-start | bytes 27656 | tf_op jit(solution)/shard_map/ppermute | solution.py:231
  365.0 0.4 collective-permute-start.87
  365.4 2.8 collective-permute-start.86
  368.3 4.3 %collective-permute-done.87 = f32[1,18,128]{2,1,0:T(8,128)S(1)} collective-permute-done((f32[1,18,128]{2,1,0:T(8,128)S(1)}, f32[1,18,128]{2,1,0:T(8,128)S(1)}, u32[]{:S(2)}, u32[]{:S(2)}) %collective-permute-start.87) | collective-permute-done | bytes 9248 | tf_op jit(solution)/shard_map/ppermute | solution.py:231
  372.9 0.6 multiply_subtract_fusion
  (73 shorter events, 1.6 us)
Async XLA Ops:
  1.4 26.2 %collective-permute-start.69 = (f32[1,18,128]{2,1,0:T(8,128)S(1)}, f32[1,18,128]{2,1,0:T(8,128)S(1)}, u32[]{:S(2)}, u32[]{:S(2)}) collective-permute-start(f32[1,18,128]{2,1,0:T(8,128)S(1)} %reshape.55), channel_id=1, source_target_pairs={{0,7},{1,6},{2,5},{3,4},{4,3},{5,2},{6,1},{7,0},{8,15},{9,14},{10,... | collective-permute-start | bytes 27656 | tf_op jit(solution)/shard_map/ppermute | solution.py:231
  7.2 20.3 %collective-permute-start.68 = (f32[1,18,128]{2,1,0:T(8,128)S(1)}, f32[1,18,128]{2,1,0:T(8,128)S(1)}, u32[]{:S(2)}, u32[]{:S(2)}) collective-permute-start(f32[1,18,128]{2,1,0:T(8,128)S(1)} %reshape.55), channel_id=1, source_target_pairs={{0,6},{1,7},{2,4},{3,5},{4,2},{5,3},{6,0},{7,1},{8,14},{9,15},{10,... | collective-permute-start | bytes 27656 | tf_op jit(solution)/shard_map/ppermute | solution.py:231
  7.7 19.9 %collective-permute-start.67 = (f32[1,18,128]{2,1,0:T(8,128)S(1)}, f32[1,18,128]{2,1,0:T(8,128)S(1)}, u32[]{:S(2)}, u32[]{:S(2)}) collective-permute-start(f32[1,18,128]{2,1,0:T(8,128)S(1)} %reshape.55), channel_id=1, source_target_pairs={{0,5},{1,4},{2,7},{3,6},{4,1},{5,0},{6,3},{7,2},{8,13},{9,12},{10,... | collective-permute-start | bytes 27656 | tf_op jit(solution)/shard_map/ppermute | solution.py:231
  11.8 15.7 %collective-permute-start.66 = (f32[1,18,128]{2,1,0:T(8,128)S(1)}, f32[1,18,128]{2,1,0:T(8,128)S(1)}, u32[]{:S(2)}, u32[]{:S(2)}) collective-permute-start(f32[1,18,128]{2,1,0:T(8,128)S(1)} %reshape.55), channel_id=1, source_target_pairs={{0,4},{1,5},{2,6},{3,7},{4,0},{5,1},{6,2},{7,3},{8,12},{9,13},{10,... | collective-permute-start | bytes 27656 | tf_op jit(solution)/shard_map/ppermute | solution.py:231
  13.6 3.7 collective-permute-start.63
  17.3 4.7 %collective-permute-start.64 = (f32[1,18,128]{2,1,0:T(8,128)S(1)}, f32[1,18,128]{2,1,0:T(8,128)S(1)}, u32[]{:S(2)}, u32[]{:S(2)}) collective-permute-start(f32[1,18,128]{2,1,0:T(8,128)S(1)} %reshape.55), channel_id=1, source_target_pairs={{0,2},{1,3},{2,0},{3,1},{4,6},{5,7},{6,4},{7,5},{8,10},{9,11},{10,... | collective-permute-start | bytes 27656 | tf_op jit(solution)/shard_map/ppermute | solution.py:231
  22.0 5.5 %collective-permute-start.65 = (f32[1,18,128]{2,1,0:T(8,128)S(1)}, f32[1,18,128]{2,1,0:T(8,128)S(1)}, u32[]{:S(2)}, u32[]{:S(2)}) collective-permute-start(f32[1,18,128]{2,1,0:T(8,128)S(1)} %reshape.55), channel_id=1, source_target_pairs={{0,3},{1,2},{2,1},{3,0},{4,7},{5,6},{6,5},{7,4},{8,11},{9,10},{10,... | collective-permute-start | bytes 27656 | tf_op jit(solution)/shard_map/ppermute | solution.py:231
  27.6 4.7 %collective-permute-start.70 = (f32[8,18,128]{2,1,0:T(8,128)S(1)}, f32[8,18,128]{2,1,0:T(8,128)S(1)}, u32[]{:S(2)}, u32[]{:S(2)}) collective-permute-start(f32[8,18,128]{2,1,0:T(8,128)S(1)} %get-tuple-element.183), channel_id=1, source_target_pairs={{0,16},{1,17},{2,18},{3,19},{4,20},{5,21},{6,22},{7,23},{8,24},{9,... | collective-permute-start | bytes 221192 | tf_op jit(solution)/shard_map/ppermute | solution.py:231
  28.2 8.3 %collective-permute-start.72 = (f32[8,18,128]{2,1,0:T(8,128)S(1)}, f32[8,18,128]{2,1,0:T(8,128)S(1)}, u32[]{:S(2)}, u32[]{:S(2)}) collective-permute-start(f32[8,18,128]{2,1,0:T(8,128)S(1)} %get-tuple-element.183), channel_id=1, source_target_pairs={{0,48},{1,49},{2,50},{3,51},{4,52},{5,53},{6,54},{7,55},{8,56},{9,... | collective-permute-start | bytes 221192 | tf_op jit(solution)/shard_map/ppermute | solution.py:231
  30.4 6.1 %collective-permute-start.71 = (f32[8,18,128]{2,1,0:T(8,128)S(1)}, f32[8,18,128]{2,1,0:T(8,128)S(1)}, u32[]{:S(2)}, u32[]{:S(2)}) collective-permute-start(f32[8,18,128]{2,1,0:T(8,128)S(1)} %get-tuple-element.183), channel_id=1, source_target_pairs={{0,32},{1,33},{2,34},{3,35},{4,36},{5,37},{6,38},{7,39},{8,40},{9,... | collective-permute-start | bytes 221192 | tf_op jit(solution)/shard_map/ppermute | solution.py:231
  36.5 11.0 %collective-permute-start.73 = (f32[32,18,128]{2,1,0:T(8,128)S(1)}, f32[32,18,128]{2,1,0:T(8,128)S(1)}, u32[]{:S(2)}, u32[]{:S(2)}) collective-permute-start(f32[32,18,128]{2,1,0:T(8,128)S(1)} %get-tuple-element.174), channel_id=1, source_target_pairs={{0,8},{1,9},{2,10},{3,11},{4,12},{5,13},{6,14},{7,15},{8,0},{9,1},... | collective-permute-start | bytes 884744 | tf_op jit(solution)/shard_map/ppermute | solution.py:231
  39.8 12.3 %collective-permute-start.74 = (f32[32,18,128]{2,1,0:T(8,128)S(1)}, f32[32,18,128]{2,1,0:T(8,128)S(1)}, u32[]{:S(2)}, u32[]{:S(2)}) collective-permute-start(f32[32,18,128]{2,1,0:T(8,128)S(1)} %get-tuple-element.174), channel_id=1, source_target_pairs={{0,128},{1,129},{2,130},{3,131},{4,132},{5,133},{6,134},{7,135},{8... | collective-permute-start | bytes 884744 | tf_op jit(solution)/shard_map/ppermute | solution.py:231
  40.5 11.7 %collective-permute-start.75 = (f32[32,18,128]{2,1,0:T(8,128)S(1)}, f32[32,18,128]{2,1,0:T(8,128)S(1)}, u32[]{:S(2)}, u32[]{:S(2)}) collective-permute-start(f32[32,18,128]{2,1,0:T(8,128)S(1)} %get-tuple-element.174), channel_id=1, source_target_pairs={{0,136},{1,137},{2,138},{3,139},{4,140},{5,141},{6,142},{7,143},{8... | collective-permute-start | bytes 884744 | tf_op jit(solution)/shard_map/ppermute | solution.py:231
  52.2 1.3 copy-start.1
  52.2 1.4 copy-start.4
  52.2 4.0 %copy-start.2 = (s32[2,4096]{1,0:T(2,128)S(1)}, s32[2,4096]{1,0:T(2,128)}, u32[]{:S(2)}) copy-start(s32[2,4096]{1,0:T(2,128)} %param.81) | copy-start | bytes 98308
  52.2 5.3 %copy-start.6 = (s32[2,1]{0,1:T(1,128)S(1)}, s32[2,1]{0,1:T(1,128)}, u32[]{:S(2)}) copy-start(s32[2,1]{0,1:T(1,128)} %param.85) | copy-start | bytes 28
  52.3 5.9 %copy-start.3 = (s32[2,8,512]{2,1,0:T(8,128)S(1)}, s32[2,8,512]{2,1,0:T(8,128)}, u32[]{:S(2)}) copy-start(s32[2,8,512]{2,1,0:T(8,128)} %param.84) | copy-start | bytes 98308
  53.5 5.6 %collective-permute-start.76 = (f32[128,18,128]{2,0,1:T(8,128)}, f32[128,18,128]{2,0,1:T(8,128)}, u32[]{:S(2)}, u32[]{:S(2)}) collective-permute-start(f32[128,18,128]{2,0,1:T(8,128)} %copy.17), channel_id=1, source_target_pairs={{0,64},{1,65},{2,66},{3,67},{4,68},{5,69},{6,70},{7,71},{8,72},{9,... | collective-permute-start | bytes 3538952 | tf_op jit(solution)/shard_map/ppermute | solution.py:231
  110.5 111.3 %collective-permute-start.53 = (f32[264,1024]{1,0:T(8,128)S(1)}, f32[264,1024]{1,0:T(8,128)}, u32[]{:S(2)}, u32[]{:S(2)}) collective-permute-start(f32[264,1024]{1,0:T(8,128)S(1)} %param.53), channel_id=1, source_target_pairs={{0,54},{1,55},{2,52},{3,53},{4,50},{5,51},{6,48},{7,49},{8,62},{9,... | collective-permute-start | bytes 3244040 | tf_op jit(solution)/shard_map/cond/branch_53_fun/ppermute | solution.py:268
  272.3 4.0 %collective-permute-start.77 = (f32[128,18,128]{2,0,1:T(8,128)}, f32[128,18,128]{2,0,1:T(8,128)}, u32[]{:S(2)}, u32[]{:S(2)}) collective-permute-start(f32[128,18,128]{2,0,1:T(8,128)} %copy.33), channel_id=1, source_target_pairs={{0,64},{1,65},{2,66},{3,67},{4,68},{5,69},{6,70},{7,71},{8,72},{9,... | collective-permute-start | bytes 3538952 | tf_op jit(solution)/shard_map/ppermute | solution.py:231
  278.4 35.4 %collective-permute-start.78 = (f32[32,18,128]{2,1,0:T(8,128)S(1)}, f32[32,18,128]{2,1,0:T(8,128)S(1)}, u32[]{:S(2)}, u32[]{:S(2)}) collective-permute-start(f32[32,18,128]{2,1,0:T(8,128)S(1)} %get-tuple-element.160), channel_id=1, source_target_pairs={{0,8},{1,9},{2,10},{3,11},{4,12},{5,13},{6,14},{7,15},{8,0},{9,1},... | collective-permute-start | bytes 884744 | tf_op jit(solution)/shard_map/ppermute | solution.py:231
  290.0 38.0 %collective-permute-start.80 = (f32[32,18,128]{2,1,0:T(8,128)S(1)}, f32[32,18,128]{2,1,0:T(8,128)S(1)}, u32[]{:S(2)}, u32[]{:S(2)}) collective-permute-start(f32[32,18,128]{2,1,0:T(8,128)S(1)} %get-tuple-element.161), channel_id=1, source_target_pairs={{0,136},{1,137},{2,138},{3,139},{4,140},{5,141},{6,142},{7,143},{8... | collective-permute-start | bytes 884744 | tf_op jit(solution)/shard_map/ppermute | solution.py:231
  313.8 15.2 %collective-permute-start.79 = (f32[32,18,128]{2,1,0:T(8,128)S(1)}, f32[32,18,128]{2,1,0:T(8,128)S(1)}, u32[]{:S(2)}, u32[]{:S(2)}) collective-permute-start(f32[32,18,128]{2,1,0:T(8,128)S(1)} %get-tuple-element.162), channel_id=1, source_target_pairs={{0,128},{1,129},{2,130},{3,131},{4,132},{5,133},{6,134},{7,135},{8... | collective-permute-start | bytes 884744 | tf_op jit(solution)/shard_map/ppermute | solution.py:231
  329.1 43.8 %copy-start = (f32[9,256]{1,0:T(8,128)S(1)}, f32[9,256]{1,0:T(8,128)}, u32[]{:S(2)}) copy-start(f32[9,256]{1,0:T(8,128)} %param.79) | copy-start | bytes 27652
  329.1 43.8 %copy-start.5 = (f32[9,256]{1,0:T(8,128)S(1)}, f32[9,256]{1,0:T(8,128)}, u32[]{:S(2)}) copy-start(f32[9,256]{1,0:T(8,128)} %param.80) | copy-start | bytes 27652
  329.2 18.4 %collective-permute-start.81 = (f32[8,18,128]{2,1,0:T(8,128)S(1)}, f32[8,18,128]{2,1,0:T(8,128)S(1)}, u32[]{:S(2)}, u32[]{:S(2)}) collective-permute-start(f32[8,18,128]{2,1,0:T(8,128)S(1)} %get-tuple-element.163), channel_id=1, source_target_pairs={{0,16},{1,17},{2,18},{3,19},{4,20},{5,21},{6,22},{7,23},{8,24},{9,... | collective-permute-start | bytes 221192 | tf_op jit(solution)/shard_map/ppermute | solution.py:231
  344.6 5.1 %collective-permute-start.83 = (f32[8,18,128]{2,1,0:T(8,128)S(1)}, f32[8,18,128]{2,1,0:T(8,128)S(1)}, u32[]{:S(2)}, u32[]{:S(2)}) collective-permute-start(f32[8,18,128]{2,1,0:T(8,128)S(1)} %get-tuple-element.164), channel_id=1, source_target_pairs={{0,48},{1,49},{2,50},{3,51},{4,52},{5,53},{6,54},{7,55},{8,56},{9,... | collective-permute-start | bytes 221192 | tf_op jit(solution)/shard_map/ppermute | solution.py:231
  345.1 6.2 %collective-permute-start.82 = (f32[8,18,128]{2,1,0:T(8,128)S(1)}, f32[8,18,128]{2,1,0:T(8,128)S(1)}, u32[]{:S(2)}, u32[]{:S(2)}) collective-permute-start(f32[8,18,128]{2,1,0:T(8,128)S(1)} %get-tuple-element.165), channel_id=1, source_target_pairs={{0,32},{1,33},{2,34},{3,35},{4,36},{5,37},{6,38},{7,39},{8,40},{9,... | collective-permute-start | bytes 221192 | tf_op jit(solution)/shard_map/ppermute | solution.py:231
  351.4 14.0 %collective-permute-start.84 = (f32[1,18,128]{2,1,0:T(8,128)S(1)}, f32[1,18,128]{2,1,0:T(8,128)S(1)}, u32[]{:S(2)}, u32[]{:S(2)}) collective-permute-start(f32[1,18,128]{2,1,0:T(8,128)S(1)} %get-tuple-element.166), channel_id=1, source_target_pairs={{0,1},{1,0},{2,3},{3,2},{4,5},{5,4},{6,7},{7,6},{8,9},{9,8},{10,11... | collective-permute-start | bytes 27656 | tf_op jit(solution)/shard_map/ppermute | solution.py:231
  355.4 12.8 %collective-permute-start.90 = (f32[1,18,128]{2,1,0:T(8,128)S(1)}, f32[1,18,128]{2,1,0:T(8,128)S(1)}, u32[]{:S(2)}, u32[]{:S(2)}) collective-permute-start(f32[1,18,128]{2,1,0:T(8,128)S(1)} %get-tuple-element.167), channel_id=1, source_target_pairs={{0,7},{1,6},{2,5},{3,4},{4,3},{5,2},{6,1},{7,0},{8,15},{9,14},{10,... | collective-permute-start | bytes 27656 | tf_op jit(solution)/shard_map/ppermute | solution.py:231
  359.1 9.1 %collective-permute-start.89 = (f32[1,18,128]{2,1,0:T(8,128)S(1)}, f32[1,18,128]{2,1,0:T(8,128)S(1)}, u32[]{:S(2)}, u32[]{:S(2)}) collective-permute-start(f32[1,18,128]{2,1,0:T(8,128)S(1)} %get-tuple-element.168), channel_id=1, source_target_pairs={{0,6},{1,7},{2,4},{3,5},{4,2},{5,3},{6,0},{7,1},{8,14},{9,15},{10,... | collective-permute-start | bytes 27656 | tf_op jit(solution)/shard_map/ppermute | solution.py:231
  359.1 9.1 %collective-permute-start.88 = (f32[1,18,128]{2,1,0:T(8,128)S(1)}, f32[1,18,128]{2,1,0:T(8,128)S(1)}, u32[]{:S(2)}, u32[]{:S(2)}) collective-permute-start(f32[1,18,128]{2,1,0:T(8,128)S(1)} %get-tuple-element.169), channel_id=1, source_target_pairs={{0,5},{1,4},{2,7},{3,6},{4,1},{5,0},{6,3},{7,2},{8,13},{9,12},{10,... | collective-permute-start | bytes 27656 | tf_op jit(solution)/shard_map/ppermute | solution.py:231
  365.0 7.6 %collective-permute-start.87 = (f32[1,18,128]{2,1,0:T(8,128)S(1)}, f32[1,18,128]{2,1,0:T(8,128)S(1)}, u32[]{:S(2)}, u32[]{:S(2)}) collective-permute-start(f32[1,18,128]{2,1,0:T(8,128)S(1)} %get-tuple-element.170), channel_id=1, source_target_pairs={{0,4},{1,5},{2,6},{3,7},{4,0},{5,1},{6,2},{7,3},{8,12},{9,13},{10,... | collective-permute-start | bytes 27656 | tf_op jit(solution)/shard_map/ppermute | solution.py:231
  365.4 7.2 %collective-permute-start.86 = (f32[1,18,128]{2,1,0:T(8,128)S(1)}, f32[1,18,128]{2,1,0:T(8,128)S(1)}, u32[]{:S(2)}, u32[]{:S(2)}) collective-permute-start(f32[1,18,128]{2,1,0:T(8,128)S(1)} %get-tuple-element.171), channel_id=1, source_target_pairs={{0,3},{1,2},{2,1},{3,0},{4,7},{5,6},{6,5},{7,4},{8,11},{9,10},{10,... | collective-permute-start | bytes 27656 | tf_op jit(solution)/shard_map/ppermute | solution.py:231
  368.2 4.6 %collective-permute-start.85 = (f32[1,18,128]{2,1,0:T(8,128)S(1)}, f32[1,18,128]{2,1,0:T(8,128)S(1)}, u32[]{:S(2)}, u32[]{:S(2)}) collective-permute-start(f32[1,18,128]{2,1,0:T(8,128)S(1)} %get-tuple-element.172), channel_id=1, source_target_pairs={{0,2},{1,3},{2,0},{3,1},{4,6},{5,7},{6,4},{7,5},{8,10},{9,11},{10,... | collective-permute-start | bytes 27656 | tf_op jit(solution)/shard_map/ppermute | solution.py:231
